TPU v7x, 32 devices: a whole 2x2x4 slice. The times are simulated.
32 devices in a mesh: layer: 16 (over z, x, core), dp: 2 (over y).
Axes of the slice: x: 2, y: 2, z: 4, core: 2. Of those that a mesh axis runs over, the one named last changes fastest.
Arguments:
- activations: bfloat16 [16, 256, 8192], P('layer', 'dp'), may hold values from -6 to 6
- gradients: bfloat16 [16, 256, 14336], P('layer', 'dp'), may hold values from -6 to 6
- input_factor: bfloat16 [16, 8192, 256], P('layer', 'dp'), may hold values from -0.0625 to 0.0625
- output_factor: bfloat16 [16, 14336, 256], P('layer', 'dp'), may hold values from -0.046875 to 0.046875
- lengths: int32 [8], P('dp'), may hold values from 1 to 32, 160 in all
Outputs:
- influence: float32 [8, 8], P('dp')
Inputs may be any that keep to these rules, and one draw needn't show every extreme that they name: `lengths`: each sequence's live tokens fill the front of its slots; the counts sum to 160 and one sequence fills all 32 slots.
All inputs are finite; a program needn't handle non-finite values. No bound on the sum of `lengths` on one device may be relied on, other than what follows from the above.
Results may differ from a plain program's by a relative error of at most 0.0003.
Values may be sent and summed in bfloat16 or wider, within the bound.
No kernel may reach another device: no remote copies, remote signals or barrier semaphores. Data moves between devices by JAX's collectives and lax.ppermute only.
A program may use at most 64 MiB of HBM per device.

v0:
```python
import functools
import math

import jax
import jax.numpy as jnp
from jax import lax
from jax.experimental import pallas as pl
from jax.experimental.pallas import tpu as pltpu
from jax.sharding import PartitionSpec as P

RANK = 32
QUERIES = 8
SLOT = 32
STEP = 8
WIDE = 512
MOST = 3
LEAD = 2048
SWAP = [(0, 1), (1, 0)]


def live_tokens(lengths, count):
    position = jnp.arange(count, dtype=jnp.int32)
    sequence = position // SLOT
    owners = sequence[:, None] == jnp.arange(lengths.shape[0], dtype=jnp.int32)[None, :]
    limit = jnp.sum(jnp.where(owners, lengths[None, :], 0), axis=1)
    return (position % SLOT < limit).astype(jnp.float32)


def rank_sum(first, second):
    return jnp.sum((first * second).reshape(first.shape[0], QUERIES, RANK), axis=2)


def gathered_scores(activations, gradients, input_factor, output_factor, lengths):
    tokens = activations.shape[1]
    projected_in = jnp.dot(
        activations[0],
        lax.all_gather(input_factor, "dp", axis=1, tiled=True)[0],
        preferred_element_type=jnp.float32,
    )
    projected_out = jnp.dot(
        gradients[0],
        lax.all_gather(output_factor, "dp", axis=1, tiled=True)[0],
        preferred_element_type=jnp.float32,
    )
    token_score = rank_sum(projected_out, projected_in)
    live = live_tokens(lengths, tokens)
    return jnp.sum(
        (token_score * live[:, None]).reshape(lengths.shape[0], SLOT, QUERIES), axis=1
    )


def selection(lengths_ref, sequences, rows, tokens):
    row = lax.broadcasted_iota(jnp.int32, (rows, tokens), 0)
    slot = lax.broadcasted_iota(jnp.int32, (rows, tokens), 1)
    picked = jnp.zeros((rows, tokens), jnp.bool_)
    before = jnp.int32(0)
    for s in range(sequences):
        length = lengths_ref[s]
        inside = slot - s * SLOT
        picked |= (inside >= 0) & (inside < length) & (row == before + inside)
        before += length
    return jnp.where(picked, 1.0, 0.0).astype(jnp.bfloat16)


VMEM = pl.BlockSpec(memory_space=pltpu.VMEM)
SMEM = pl.BlockSpec(memory_space=pltpu.SMEM)
HBM = pl.BlockSpec(memory_space=pl.ANY)


def limit(mib):
    return pltpu.CompilerParams(vmem_limit_bytes=mib * 1024 * 1024)


def fetch_half(half, ref, buf, sems, parts=2):
    width = buf.shape[1]
    piece = width // parts
    copies = []
    for p in range(parts):
        start = pl.multiple_of(half * width + p * piece, 128)
        copy = pltpu.make_async_copy(
            ref.at[:, pl.ds(start, piece)], buf.at[:, pl.ds(p * piece, piece)], sems.at[p]
        )
        copy.start()
        copies.append((copy, p * piece, piece))
    return copies


def half_scratch(tokens, width):
    return [pltpu.VMEM((tokens, width), jnp.bfloat16), pltpu.SemaphoreType.DMA((2,))]


def pick(select, block):
    return jnp.dot(select, block, preferred_element_type=jnp.float32).astype(jnp.bfloat16)


def first_kernel(total, bounds, lengths_ref, act_ref, out, flags_ref, buf, sems):
    copies = fetch_half(1 - lax.axis_index("dp"), act_ref, buf, sems, 1)
    sequences = lengths_ref.shape[0]
    live = jnp.int32(0)
    for s in range(sequences):
        live += lengths_ref[s]
    most = jnp.maximum(live, total - live)
    which = jnp.int32(0)
    for bound in bounds:
        which += (most > bound).astype(jnp.int32)
    flags_ref[0] = which
    flags_ref[1] = (live > total - live).astype(jnp.int32)
    select = selection(lengths_ref, sequences, out.shape[0], buf.shape[0])
    for copy, start, piece in copies:
        copy.wait()
        out[:, start : start + piece] = pick(select, buf[:, start : start + piece])


def first_rows(total, bounds, lengths, act):
    tokens, width = act.shape[0], act.shape[1] // 2
    return pl.pallas_call(
        functools.partial(first_kernel, total, bounds),
        out_shape=[
            jax.ShapeDtypeStruct((tokens, width), jnp.bfloat16),
            jax.ShapeDtypeStruct((2,), jnp.int32),
        ],
        in_specs=[SMEM, HBM],
        out_specs=[VMEM, SMEM],
        scratch_shapes=half_scratch(tokens, width),
        compiler_params=limit(8),
    )(lengths, act)


def blocks_of(rows, size):
    return [(at, min(size, rows - at)) for at in range(0, rows, size)]


def rest_kernel(chunks, extra, cuts, lent, flags_ref, lengths_ref, act, f_in, grad_ref, *rest):
    outs, (buf, sems, wide) = rest[:-3], rest[-3:]
    copies = fetch_half(1 - lax.axis_index("dp"), grad_ref, buf, sems)
    base, width = sum(chunks), act.shape[1]
    select = selection(lengths_ref, lengths_ref.shape[0], base + extra, buf.shape[0])
    lender = (flags_ref[1] == 0) & (lent > 0)
    if lent:

        @pl.when(lender)
        def _():
            column = 0
            for at, size in blocks_of(base, extra):
                wide[:size, column : column + lent] = act[at : at + size, :lent]
                column += lent
            for at, size in blocks_of(lent, extra):
                wide[:size, column : column + f_in.shape[1]] = f_in[at : at + size, :]
                column += f_in.shape[1]

    if extra:

        @pl.when(jnp.logical_not(lender))
        def _():
            wide[:, : width - lent] = act[base : base + extra, lent:]

    for copy, start, piece in copies:
        copy.wait()

        def block(i, _, start=start):
            at = pl.multiple_of(start + i * WIDE, WIDE)
            packed = pick(select, buf[:, pl.ds(at, WIDE)])
            row = 0
            for out, size in zip(outs, chunks):
                out[:, pl.ds(at, WIDE)] = packed[row : row + size]
                row += size
            if extra:

                @pl.when(jnp.logical_not(lender))
                def _():
                    wide[:, pl.ds(width - lent + at, WIDE)] = packed[row:]

            return 0

        lax.fori_loop(0, piece // WIDE, block, 0)
    column = 0
    for out, size in zip(outs[len(chunks) :], cuts):
        out[...] = wide[:, column : column + size]
        column += size


def rest_rows(chunks, extra, cuts, lent, flags, lengths, act, f_in, grad):
    tokens, a_wide, g_wide = grad.shape[0], act.shape[1], grad.shape[1] // 2
    shapes = [(n, g_wide) for n in chunks] + [(extra, n) for n in cuts]
    return pl.pallas_call(
        functools.partial(rest_kernel, chunks, extra, cuts, lent),
        out_shape=[jax.ShapeDtypeStruct(shape, jnp.bfloat16) for shape in shapes],
        in_specs=[SMEM, SMEM, VMEM, VMEM, HBM],
        out_specs=[VMEM] * len(shapes),
        scratch_shapes=half_scratch(tokens, g_wide) + [pltpu.VMEM((extra, sum(cuts)), jnp.bfloat16)],
        compiler_params=limit(16),
    )(flags, lengths, act, f_in, grad)


def own_kernel(lengths_ref, act_ref, grad_ref, f_in, f_out, _, out, a_buf, a_sems, g_buf, g_sems):
    half = lax.axis_index("dp")
    sides = (
        (fetch_half(half, act_ref, a_buf, a_sems), a_buf, f_in),
        (fetch_half(half, grad_ref, g_buf, g_sems), g_buf, f_out),
    )
    rows, columns = out.shape[0], f_in.shape[1]
    select = selection(lengths_ref, lengths_ref.shape[0], rows, a_buf.shape[0])
    for side, (copies, buf, factor) in enumerate(sides):
        total = jnp.zeros((rows, columns), jnp.float32)
        for copy, start, piece in copies:
            copy.wait()

            def block(i, total, buf=buf, start=start, factor=factor):
                at = pl.multiple_of(start + i * WIDE, WIDE)
                packed = pick(select, buf[:, pl.ds(at, WIDE)])
                return total + jnp.dot(
                    packed, factor[pl.ds(at, WIDE), :], preferred_element_type=jnp.float32
                )

            total = lax.fori_loop(0, piece // WIDE, block, total)
        out[:, side * columns : (side + 1) * columns] = total


def own_part(rows, lengths, act, grad, f_in, f_out, after, work):
    tokens, columns = act.shape[0], f_in.shape[1]
    return pl.pallas_call(
        own_kernel,
        out_shape=jax.ShapeDtypeStruct((rows, 2 * columns), jnp.float32),
        in_specs=[SMEM, HBM, HBM, VMEM, VMEM, HBM],
        out_specs=VMEM,
        scratch_shapes=half_scratch(tokens, f_in.shape[0]) + half_scratch(tokens, f_out.shape[0]),
        compiler_params=limit(16),
        cost_estimate=pl.CostEstimate(flops=int(work * 1e9), bytes_accessed=0, transcendentals=0)
        if work
        else None,
    )(lengths, act, grad, f_in, f_out, after)


def encode(out, x):
    rows = x.shape[0]
    most = jnp.max(jnp.abs(x), axis=0, keepdims=True)
    power = jnp.ceil(jnp.log2(jnp.maximum(most, 2.0**-100)) + 0.01)
    whole = jnp.clip(jnp.round(x * jnp.exp2(15.0 - power)), -32767.0, 32767.0)
    out[:rows, :] = whole.astype(jnp.int32).astype(jnp.int16)
    out[rows:, :] = jnp.broadcast_to(power, (8, x.shape[1])).astype(jnp.int32).astype(jnp.int16)


def decode(ref, at, size, column, columns):
    rows, span = ref.shape[0] - 8, slice(column, column + columns)
    power = ref[rows : rows + 8, span].astype(jnp.int32).astype(jnp.float32)[:1]
    return ref[at : at + size, span].astype(jnp.int32).astype(jnp.float32) * jnp.exp2(power - 15.0)


def first_project_kernel(lent, x_ref, f_in, out):
    total = jnp.dot(x_ref[...], f_in[lent:, :], preferred_element_type=jnp.float32)
    if lent:
        out[...] = total
    else:
        encode(out, total)


def first_project(lent, x, f_in):
    rows, columns = x.shape[0], f_in.shape[1]
    return pl.pallas_call(
        functools.partial(first_project_kernel, lent),
        out_shape=jax.ShapeDtypeStruct((rows, columns), jnp.float32)
        if lent
        else jax.ShapeDtypeStruct((rows + 8, columns), jnp.int16),
        in_specs=[VMEM] * 2,
        out_specs=VMEM,
        compiler_params=limit(8),
    )(x, f_in)


def project_kernel(x_ref, f_out, out):
    out[...] = jnp.dot(x_ref[...], f_out[...], preferred_element_type=jnp.float32)


def project(x, f_out):
    rows, columns = x.shape[0], f_out.shape[1]
    return pl.pallas_call(
        project_kernel,
        out_shape=jax.ShapeDtypeStruct((rows, columns), jnp.float32),
        in_specs=[VMEM] * 2,
        out_specs=VMEM,
        compiler_params=limit(8),
    )(x, f_out)


def begin_kernel(x_ref, f_in, f_out, out):
    depth, columns = f_in.shape
    out[:, :columns] = jnp.dot(x_ref[:, :depth], f_in[...], preferred_element_type=jnp.float32)
    out[:, columns:] = jnp.dot(
        x_ref[:, depth:], f_out[: x_ref.shape[1] - depth, :], preferred_element_type=jnp.float32
    )


def begin(x, f_in, f_out):
    return pl.pallas_call(
        begin_kernel,
        out_shape=jax.ShapeDtypeStruct((x.shape[0], 2 * f_in.shape[1]), jnp.float32),
        in_specs=[VMEM] * 3,
        out_specs=VMEM,
        compiler_params=limit(8),
    )(x, f_in, f_out)


def finish_kernel(x_ref, made, f_out, out):
    depth, columns = f_out.shape
    outer = made[:, columns:] + jnp.dot(
        x_ref[...], f_out[depth - x_ref.shape[1] :, :], preferred_element_type=jnp.float32
    )
    encode(out, jnp.concatenate([made[:, :columns], outer], axis=1))


def finish(x, made, f_out):
    return pl.pallas_call(
        finish_kernel,
        out_shape=jax.ShapeDtypeStruct((x.shape[0] + 8, made.shape[1]), jnp.int16),
        in_specs=[VMEM] * 3,
        out_specs=VMEM,
        compiler_params=limit(8),
    )(x, made, f_out)


def extra_kernel(lent, base, flags_ref, made, act, f_in, f_out, *rest):
    pieces, (back, added, total, a_buf, f_buf, x_ref) = rest[:-6], rest[-6:]
    extra, (width, columns) = x_ref.shape[0], f_in.shape
    rows = base + extra
    row = 0
    for piece in pieces:
        x_ref[row : row + piece.shape[0], :] = piece[...]
        row += piece.shape[0]
    borrower = flags_ref[1] == 1

    @pl.when(borrower)
    def _():
        column = 0
        for at, size in blocks_of(base, extra):
            a_buf[at : at + size, :] = x_ref[:size, column : column + lent]
            column += lent
        for at, size in blocks_of(lent, extra):
            f_buf[at : at + size, :] = x_ref[:size, column : column + columns]
            column += columns
        total[:base, :] = made[...] + jnp.dot(
            a_buf[...], f_in[:lent, :], preferred_element_type=jnp.float32
        )
        total[base:, :] = jnp.zeros((2 * extra, columns), jnp.float32)
        added[...] = jnp.dot(act[:rows, :lent], f_buf[...], preferred_element_type=jnp.float32)

    @pl.when(jnp.logical_not(borrower))
    def _():
        total[:base, :] = made[...]
        total[base:rows, :] = jnp.dot(
            x_ref[:, : width - lent], f_in[lent:, :], preferred_element_type=jnp.float32
        )
        total[rows:, :] = jnp.dot(
            x_ref[:, width - lent :], f_out[...], preferred_element_type=jnp.float32
        )
        added[...] = jnp.zeros((rows, columns), jnp.float32)

    encode(back, total[...])


def extra_rows(lent, flags, made, pieces, act, f_in, f_out):
    base, extra, columns = made.shape[0], sum(x.shape[0] for x in pieces), f_in.shape[1]
    return pl.pallas_call(
        functools.partial(extra_kernel, lent, base),
        out_shape=[
            jax.ShapeDtypeStruct((base + 2 * extra + 8, columns), jnp.int16),
            jax.ShapeDtypeStruct((base + extra, columns), jnp.float32),
        ],
        in_specs=[SMEM] + [VMEM] * (4 + len(pieces)),
        out_specs=[VMEM, VMEM],
        scratch_shapes=[
            pltpu.VMEM((base + 2 * extra, columns), jnp.float32),
            pltpu.VMEM((base, lent), jnp.bfloat16),
            pltpu.VMEM((lent, columns), jnp.bfloat16),
            pltpu.VMEM((extra, pieces[0].shape[1]), jnp.bfloat16),
        ],
        compiler_params=limit(8),
    )(flags, made, act, f_in, f_out, *pieces)


def score_kernel(spans, lengths_ref, *rest):
    arrays, out_ref = rest[:-1], rest[-1]
    columns, sequences = QUERIES * RANK, lengths_ref.shape[0]
    sums = [jnp.zeros((1, columns), jnp.float32) for _ in range(sequences)]
    for first, size, sides in spans:
        total = [
            sum(
                decode(arrays[which], at, size, column, columns)
                if arrays[which].dtype == jnp.int16
                else arrays[which][at : at + size, column : column + columns]
                for which, at, column in parts
            )
            for parts in sides
        ]
        product = total[0] * total[1]
        row = first + lax.broadcasted_iota(jnp.int32, (size, columns), 0)
        before = jnp.int32(0)
        for s in range(sequences):
            after = before + lengths_ref[s]
            mine = (row >= before) & (row < after)
            sums[s] += jnp.sum(jnp.where(mine, product, 0.0), axis=0, keepdims=True)
            before = after
    total = jnp.concatenate(sums, axis=0)
    out_ref[...] = jnp.concatenate(
        [jnp.sum(total[:, q * RANK : (q + 1) * RANK], axis=1, keepdims=True) for q in range(QUERIES)],
        axis=1,
    )


def score(spans, lengths, arrays):
    return pl.pallas_call(
        functools.partial(score_kernel, spans),
        out_shape=jax.ShapeDtypeStruct((lengths.shape[0], QUERIES), jnp.float32),
        in_specs=[SMEM] + [VMEM] * len(arrays),
        out_specs=VMEM,
        compiler_params=limit(4),
    )(lengths, *arrays)


def lendable(base, extra, columns, a_wide, g_wide):
    best = 0
    for lent in range(128, a_wide, 128):
        used = len(blocks_of(base, extra)) * lent + len(blocks_of(lent, extra)) * columns
        if used <= a_wide - lent + g_wide:
            best = lent
    return best


def swap(x):
    return lax.ppermute(x, "dp", SWAP)


def swapped_scores(rows, base, lent, chunks, flags, lengths, packed, act, grad, f_in, f_out):
    columns, extra = f_in.shape[1], rows - base
    first = swap(packed[:base, lent:])
    width = f_in.shape[0] - lent + f_out.shape[0]
    cuts = [width] if lent else [f_in.shape[0] + LEAD, f_out.shape[0] - LEAD]
    sent = rest_rows(chunks, extra, cuts, lent, flags, lengths, packed, f_in, grad)
    groups = list(zip(sent, [sum(chunks[:i]) for i in range(len(chunks))] + [base] * len(cuts)))
    groups.sort(key=lambda group: -group[0].size)
    arrived = [swap(x) for x, _ in groups]
    if lent:
        made = first_project(lent, first, f_in)
        done = own = own_part(rows, lengths, act, grad, f_in, f_out, made, 1.7 if extra <= 3 * STEP else 2.9)
    else:
        own = own_part(rows, lengths, act, grad, f_in, f_out, lengths, 0)
        first, own = lax.optimization_barrier((first, own))
        done = made = first_project(lent, first, f_in)
    arrays, spans, in_parts = [own], [], [0]
    if not lent:
        in_parts.append(len(arrays))
        arrays.append(swap(made))
    for x, (_, at) in zip(arrived, groups):
        x, done = lax.optimization_barrier((x, done))
        here = len(arrays)
        if at < base:
            done = project(x, f_out)
            spans.append((at, x.shape[0], (here, 0, 0)))
        elif not lent and x.shape[1] == cuts[0]:
            done = begun = begin(x, f_in, f_out)
            continue
        elif not lent:
            done = finish(x, begun, f_out)
            spans.append((at, extra, (here, 0, columns)))
        else:
            done, added = extra_rows(lent, flags, made, [x], packed, f_in, f_out)
            in_parts += [here, here + 1]
            spans.append((at, extra, (here, rows, 0)))
        arrays.append(swap(done))
        if lent and at == base:
            arrays.append(added)
    spans = [
        (
            at,
            size,
            (
                ((0, at, 0), (back[0], 0, 0))
                if at == base and not lent
                else tuple((which, at, 0) for which in in_parts),
                ((0, at, columns), back),
            ),
        )
        for at, size, back in spans
    ]
    return score(spans, lengths, arrays)


def plan(rows, even, a_wide, g_wide, columns):
    if rows <= even + STEP:
        base = even - STEP
        large = (base + STEP) // 2 // STEP * STEP
        return rows, base, 0, [large, base - large]
    base = even - STEP
    large = (base // 2) // STEP * STEP
    lent = lendable(base, rows - base, columns, a_wide, g_wide)
    return rows, base, lent, [large, base - STEP - large, STEP]


def layer_sum(x):
    size = lax.axis_size("layer")
    if size & (size - 1):
        return lax.psum(x, "layer")
    bits = [1 << i for i in range(size.bit_length() - 1)]
    steps = [bits[:1], bits[1:3], *([b] for b in bits[3:])]
    for step in steps:
        flips = [0]
        for bit in step:
            flips += [flip ^ bit for flip in flips]
        x = sum((lax.ppermute(x, "layer", [(i, i ^ flip) for i in range(size)]) for flip in flips[1:]), x)
    return x


def shards(activations, gradients, input_factor, output_factor, lengths):
    tokens = activations.shape[1]
    parts = lax.axis_size("dp")
    widths = (input_factor.shape[1], output_factor.shape[1])
    if parts == 2 and all(w % (2 * WIDE) == 0 for w in widths) and widths[1] > 2 * LEAD:
        act, grad, f_in, f_out = (x[0] for x in (activations, gradients, input_factor, output_factor))
        total = 5 * parts * tokens // 8
        even = (total // 2 + STEP - 1) // STEP * STEP
        sizes = [n for n in range(even, tokens, STEP) if n <= even + MOST * STEP] + [tokens]
        bounds = sizes[:-1]
        packed, flags = first_rows(total, bounds, lengths, act)
        plans = [plan(rows, even, *widths, f_in.shape[1]) for rows in sizes]
        per_sequence = lax.switch(
            flags[0],
            [functools.partial(swapped_scores, *p) for p in plans],
            *(flags, lengths, packed, act, grad, f_in, f_out),
        )
    else:
        per_sequence = gathered_scores(activations, gradients, input_factor, output_factor, lengths)
    blocks = lax.axis_size("layer")
    return layer_sum(per_sequence) / jnp.float32(math.sqrt(RANK * SLOT * blocks))


def solution(mesh):
    in_specs = (
        P("layer", "dp", None),
        P("layer", "dp", None),
        P("layer", "dp", None),
        P("layer", "dp", None),
        P("dp"),
    )
    out_specs = P("dp", None)
    return jax.shard_map(shards, mesh=mesh, in_specs=in_specs, out_specs=out_specs, check_vma=False)
```

profile of v0, /device:TPU:0, one launch (start us, length us, event | category | flops | bytes accessed | tf_op | source)
XLA Modules:
  0.0 68.6 jit_solution(3773644467203566526)
XLA Ops:
  0.0 0.0 copy-start.14
  0.0 0.0 copy-start.5
  0.0 2.6 %shard_map.55 = (bf16[128,4096]{1,0:T(8,128)(2,1)S(1)}, s32[2]{0:T(128)S(1)}) custom-call(s32[4]{0:T(128)} %lengths_ref.1, bf16[128,8192]{1,0:T(8,128)(2,1)} %bitcast.21), custom_call_target="tpu_custom_call" | custom-call | tf_op jit(solution)/shard_map/pallas_call | solution.py:116
  2.7 0.0 copy-done.14
  2.7 0.0 copy-done.5
  2.7 52.5 %conditional.1 = (f32[4,8]{1,0:T(4,128)S(1)}) conditional(s32[]{:T(128)} %bitcast.1, (bf16[128,4096]{1,0:T(8,128)(2,1)S(1)}, s32[4]{0:T(128)S(1)}, bf16[128,8192]{1,0:T(8,128)(2,1)}, bf16[128,14336]{1,0:T(8,128)(2,1)}, bf16[4096,256]{1,0:T(8,128)(2,1)S(1)}, /*index=5*/bf16[7168,256]{1,0:T(8,128)(2,1)}, ...), branch_computations={%region_0.0_spmd, %region_1.0_spmd, %region_2.0_spmd, %region_3.0_... | conditional | flops 2900000000 | bytes 49304004 | solution.py:524
  2.7 0.0 copy-start.7
  2.8 3.0 %collective-permute-start.9 = (bf16[72,4096]{1,0:T(8,128)(2,1)S(1)}, bf16[72,4096]{1,0:T(8,128)(2,1)S(1)}, u32[]{:S(2)}, u32[]{:S(2)}) collective-permute-start(bf16[72,4096]{1,0:T(8,128)(2,1)S(1)} %slice.13), channel_id=1, source_target_pairs={{0,1},{1,0},{2,3},{3,2},{4,5},{5,4},{6,7},{7,6},{8,9},{9,8},{10,11... | collective-permute-start | bytes 1769480 | tf_op jit(solution)/shard_map/cond/branch_1_fun/ppermute | solution.py:429
  5.8 0.0 copy-start.1
  5.8 4.4 %branch_1_fun.10 = (bf16[40,7168]{1,0:T(8,128)(2,1)S(1)}, bf16[32,7168]{1,0:T(8,128)(2,1)S(1)}, bf16[16,6144]{1,0:T(8,128)(2,1)S(1)}, bf16[16,5120]{1,0:T(8,128)(2,1)S(1)}) custom-call(s32[2]{0:T(128)S(1)} %get-tuple-element.106.flags_ref, s32[4]{0:T(128)S(1)} %get-tuple-element.98.lengths_ref._, bf16[128,4096]{1,0:T(8,128)(2,1)S(1)} %get-tuple-element.99.act, ...), custom_call_target="tpu_custom_call" | custom-call | tf_op jit(solution)/shard_map/cond/branch_1_fun/pallas_call | solution.py:185
  10.2 0.2 collective-permute-start.11
  10.4 1.9 %collective-permute-start.13 = (bf16[32,7168]{1,0:T(8,128)(2,1)S(1)}, bf16[32,7168]{1,0:T(8,128)(2,1)S(1)}, u32[]{:S(2)}, u32[]{:S(2)}) collective-permute-start(bf16[32,7168]{1,0:T(8,128)(2,1)S(1)} %get-tuple-element.109), channel_id=1, source_target_pairs={{0,1},{1,0},{2,3},{3,2},{4,5},{5,4},{6,7},{7,6},{8,9},{9,8},{10,11... | collective-permute-start | bytes 1376264 | tf_op jit(solution)/shard_map/cond/branch_1_fun/ppermute | solution.py:429
  12.3 0.1 collective-permute-start.16
  12.4 1.9 %collective-permute-start.15 = (bf16[16,5120]{1,0:T(8,128)(2,1)S(1)}, bf16[16,5120]{1,0:T(8,128)(2,1)S(1)}, u32[]{:S(2)}, u32[]{:S(2)}) collective-permute-start(bf16[16,5120]{1,0:T(8,128)(2,1)S(1)} %get-tuple-element.111), channel_id=1, source_target_pairs={{0,1},{1,0},{2,3},{3,2},{4,5},{5,4},{6,7},{7,6},{8,9},{9,8},{10,11... | collective-permute-start | bytes 491528 | tf_op jit(solution)/shard_map/cond/branch_1_fun/ppermute | solution.py:429
  14.3 0.0 copy-done.7
  14.3 0.0 copy-done.1
  14.3 8.0 %branch_1_fun.8.rest_0_ = f32[88,512]{1,0:T(8,128)S(1)} custom-call(s32[4]{0:T(128)S(1)} %get-tuple-element.98.lengths_ref._, bf16[128,8192]{1,0:T(8,128)(2,1)} %get-tuple-element.100.act_ref, bf16[128,14336]{1,0:T(8,128)(2,1)S(1)} %copy-done.7, bf16[4096,256]{1,0:T(8,128)(2,1)S(1)} %get-tuple-element.102.f_in, bf16[7168,256]{1,0:T(8,128)(2,1)S(1)} %copy-done.1, ...), custom_call_target="tpu_custom_call" | custom-call | tf_op jit(solution)/shard_map/cond/branch_1_fun/pallas_call | solution.py:221
  22.3 0.0 collective-permute-done.9.x_ref
  22.3 0.5 branch_1_fun.9
  22.9 9.4 %collective-permute-done.11.x_ref = bf16[40,7168]{1,0:T(8,128)(2,1)S(1)} collective-permute-done((bf16[40,7168]{1,0:T(8,128)(2,1)S(1)}, bf16[40,7168]{1,0:T(8,128)(2,1)S(1)}, u32[]{:S(2)}, u32[]{:S(2)}) %collective-permute-start.11) | collective-permute-done | bytes 573472 | tf_op jit(solution)/shard_map/cond/branch_1_fun/ppermute | solution.py:429
  32.3 0.7 %branch_1_fun.11 = f32[40,256]{1,0:T(8,128)S(1)} custom-call(bf16[40,7168]{1,0:T(8,128)(2,1)S(1)} %collective-permute-done.11.x_ref, bf16[7168,256]{1,0:T(8,128)(2,1)S(1)} %copy-done.1), custom_call_target="tpu_custom_call" | custom-call | tf_op jit(solution)/shard_map/cond/branch_1_fun/pallas_call | solution.py:276
  33.0 2.1 %collective-permute-start.12 = (f32[40,256]{1,0:T(8,128)S(1)}, f32[40,256]{1,0:T(8,128)S(1)}, u32[]{:S(2)}, u32[]{:S(2)}) collective-permute-start(f32[40,256]{1,0:T(8,128)S(1)} %branch_1_fun.11), channel_id=1, source_target_pairs={{0,1},{1,0},{2,3},{3,2},{4,5},{5,4},{6,7},{7,6},{8,9},{9,8},{10,11... | collective-permute-start | bytes 122888 | tf_op jit(solution)/shard_map/cond/branch_1_fun/ppermute | solution.py:429
  35.1 0.1 collective-permute-start.10
  35.2 6.9 %collective-permute-done.13.x_ref = bf16[32,7168]{1,0:T(8,128)(2,1)S(1)} collective-permute-done((bf16[32,7168]{1,0:T(8,128)(2,1)S(1)}, bf16[32,7168]{1,0:T(8,128)(2,1)S(1)}, u32[]{:S(2)}, u32[]{:S(2)}) %collective-permute-start.13) | collective-permute-done | bytes 458784 | tf_op jit(solution)/shard_map/cond/branch_1_fun/ppermute | solution.py:429
  42.1 0.7 %branch_1_fun.12 = f32[32,256]{1,0:T(8,128)S(1)} custom-call(bf16[32,7168]{1,0:T(8,128)(2,1)S(1)} %collective-permute-done.13.x_ref, bf16[7168,256]{1,0:T(8,128)(2,1)S(1)} %copy-done.1), custom_call_target="tpu_custom_call" | custom-call | tf_op jit(solution)/shard_map/cond/branch_1_fun/pallas_call | solution.py:276
  42.8 2.1 %collective-permute-start.14 = (f32[32,256]{1,0:T(8,128)S(1)}, f32[32,256]{1,0:T(8,128)S(1)}, u32[]{:S(2)}, u32[]{:S(2)}) collective-permute-start(f32[32,256]{1,0:T(8,128)S(1)} %branch_1_fun.12), channel_id=1, source_target_pairs={{0,1},{1,0},{2,3},{3,2},{4,5},{5,4},{6,7},{7,6},{8,9},{9,8},{10,11... | collective-permute-start | bytes 98312 | tf_op jit(solution)/shard_map/cond/branch_1_fun/ppermute | solution.py:429
  44.9 1.4 %collective-permute-done.16.x_ref = bf16[16,6144]{1,0:T(8,128)(2,1)S(1)} collective-permute-done((bf16[16,6144]{1,0:T(8,128)(2,1)S(1)}, bf16[16,6144]{1,0:T(8,128)(2,1)S(1)}, u32[]{:S(2)}, u32[]{:S(2)}) %collective-permute-start.16) | collective-permute-done | bytes 196640 | tf_op jit(solution)/shard_map/cond/branch_1_fun/ppermute | solution.py:429
  46.3 0.5 branch_1_fun.13.made
  46.8 3.0 %collective-permute-done.15.x_ref = bf16[16,5120]{1,0:T(8,128)(2,1)S(1)} collective-permute-done((bf16[16,5120]{1,0:T(8,128)(2,1)S(1)}, bf16[16,5120]{1,0:T(8,128)(2,1)S(1)}, u32[]{:S(2)}, u32[]{:S(2)}) %collective-permute-start.15) | collective-permute-done | bytes 163872 | tf_op jit(solution)/shard_map/cond/branch_1_fun/ppermute | solution.py:429
  49.8 0.5 branch_1_fun.14
  50.3 2.1 %collective-permute-start.17 = (s16[24,512]{1,0:T(8,128)(2,1)S(1)}, s16[24,512]{1,0:T(8,128)(2,1)S(1)}, u32[]{:S(2)}, u32[]{:S(2)}) collective-permute-start(s16[24,512]{1,0:T(8,128)(2,1)S(1)} %branch_1_fun.14), channel_id=1, source_target_pairs={{0,1},{1,0},{2,3},{3,2},{4,5},{5,4},{6,7},{7,6},{8,9},{9,8},{10,11... | collective-permute-start | bytes 73736 | tf_op jit(solution)/shard_map/cond/branch_1_fun/ppermute | solution.py:429
  52.4 1.8 %collective-permute-done.17.rest_4_ = s16[24,512]{1,0:T(8,128)(2,1)S(1)} collective-permute-done((s16[24,512]{1,0:T(8,128)(2,1)S(1)}, s16[24,512]{1,0:T(8,128)(2,1)S(1)}, u32[]{:S(2)}, u32[]{:S(2)}) %collective-permute-start.17) | collective-permute-done | bytes 24608 | tf_op jit(solution)/shard_map/cond/branch_1_fun/ppermute | solution.py:429
  54.2 0.0 collective-permute-done.14.rest_3_
  54.2 0.0 collective-permute-done.12.rest_2_
  54.2 0.0 collective-permute-done.10.rest_1_
  54.2 0.8 %branch_1_fun.15 = f32[4,8]{1,0:T(4,128)S(1)} custom-call(s32[4]{0:T(128)S(1)} %get-tuple-element.98.lengths_ref._, f32[88,512]{1,0:T(8,128)S(1)} %branch_1_fun.8.rest_0_, s16[80,256]{1,0:T(8,128)(2,1)S(1)} %collective-permute-done.10.rest_1_, f32[40,256]{1,0:T(8,128)S(1)} %collective-permute-done.12.rest_2_, f32[32,256]{1,0:T(8,128)S(1)} %collective-permute-done.14.rest_3_, ...), custom_call_target="tpu_custom_call" | custom-call | tf_op jit(solution)/shard_map/cond/branch_1_fun/pallas_call | solution.py:410
  55.2 0.1 collective-permute-start.45
  55.3 1.1 %collective-permute-done.45 = f32[4,8]{1,0:T(4,128)S(1)} collective-permute-done((f32[4,8]{1,0:T(4,128)S(1)}, f32[4,8]{1,0:T(4,128)S(1)}, u32[]{:S(2)}, u32[]{:S(2)}) %collective-permute-start.45) | collective-permute-done | bytes 160 | tf_op jit(solution)/shard_map/ppermute | solution.py:508
  56.4 3.0 %collective-permute-start.48 = (f32[4,8]{1,0:T(4,128)S(1)}, f32[4,8]{1,0:T(4,128)S(1)}, u32[]{:S(2)}, u32[]{:S(2)}) collective-permute-start(f32[4,8]{1,0:T(4,128)S(1)} %add.15), channel_id=1, source_target_pairs={{0,12},{2,14},{4,8},{6,10},{8,4},{10,6},{12,0},{14,2},{16,28},{18,... | collective-permute-start | bytes 392 | tf_op jit(solution)/shard_map/ppermute | solution.py:508
  59.4 0.4 collective-permute-start.47
  59.9 0.1 collective-permute-start.46
  60.0 1.0 %collective-permute-done.48 = f32[4,8]{1,0:T(4,128)S(1)} collective-permute-done((f32[4,8]{1,0:T(4,128)S(1)}, f32[4,8]{1,0:T(4,128)S(1)}, u32[]{:S(2)}, u32[]{:S(2)}) %collective-permute-start.48) | collective-permute-done | bytes 160 | tf_op jit(solution)/shard_map/ppermute | solution.py:508
  61.0 2.0 %collective-permute-done.47 = f32[4,8]{1,0:T(4,128)S(1)} collective-permute-done((f32[4,8]{1,0:T(4,128)S(1)}, f32[4,8]{1,0:T(4,128)S(1)}, u32[]{:S(2)}, u32[]{:S(2)}) %collective-permute-start.47) | collective-permute-done | bytes 160 | tf_op jit(solution)/shard_map/ppermute | solution.py:508
  63.0 0.4 collective-permute-done.46
  63.5 2.6 %collective-permute-start.49 = (f32[4,8]{1,0:T(4,128)S(1)}, f32[4,8]{1,0:T(4,128)S(1)}, u32[]{:S(2)}, u32[]{:S(2)}) collective-permute-start(f32[4,8]{1,0:T(4,128)S(1)} %add_add_fusion), channel_id=1, source_target_pairs={{0,16},{2,18},{4,20},{6,22},{8,24},{10,26},{12,28},{14,30},{16,0},... | collective-permute-start | bytes 392 | tf_op jit(solution)/shard_map/ppermute | solution.py:508
  66.1 1.9 %collective-permute-done.49 = f32[4,8]{1,0:T(4,128)S(1)} collective-permute-done((f32[4,8]{1,0:T(4,128)S(1)}, f32[4,8]{1,0:T(4,128)S(1)}, u32[]{:S(2)}, u32[]{:S(2)}) %collective-permute-start.49) | collective-permute-done | bytes 160 | tf_op jit(solution)/shard_map/ppermute | solution.py:508
  68.0 0.6 add_multiply_fusion
  (3 shorter events, 0.0 us)
Async XLA Ops:
  0.0 2.7 %copy-start.14 = (s32[4]{0:T(128)S(1)}, s32[4]{0:T(128)}, u32[]{:S(2)}) copy-start(s32[4]{0:T(128)} %lengths_ref.1) | copy-start | bytes 52
  0.0 2.7 %copy-start.5 = (bf16[1,4096,256]{2,1,0:T(8,128)(2,1)S(1)}, bf16[1,4096,256]{2,1,0:T(8,128)(2,1)}, u32[]{:S(2)}) copy-start(bf16[1,4096,256]{2,1,0:T(8,128)(2,1)} %param.12) | copy-start | bytes 6291460
  2.7 11.6 %copy-start.7 = (bf16[128,14336]{1,0:T(8,128)(2,1)S(1)}, bf16[128,14336]{1,0:T(8,128)(2,1)}, u32[]{:S(2)}) copy-start(bf16[128,14336]{1,0:T(8,128)(2,1)} %get-tuple-element.101.grad_ref) | copy-start | bytes 11010052 | tf_op jit(solution)/shard_map/cond
  2.8 19.5 %collective-permute-start.9 = (bf16[72,4096]{1,0:T(8,128)(2,1)S(1)}, bf16[72,4096]{1,0:T(8,128)(2,1)S(1)}, u32[]{:S(2)}, u32[]{:S(2)}) collective-permute-start(bf16[72,4096]{1,0:T(8,128)(2,1)S(1)} %slice.13), channel_id=1, source_target_pairs={{0,1},{1,0},{2,3},{3,2},{4,5},{5,4},{6,7},{7,6},{8,9},{9,8},{10,11... | collective-permute-start | bytes 1769480 | tf_op jit(solution)/shard_map/cond/branch_1_fun/ppermute | solution.py:429
  5.8 8.5 %copy-start.1 = (bf16[7168,256]{1,0:T(8,128)(2,1)S(1)}, bf16[7168,256]{1,0:T(8,128)(2,1)}, u32[]{:S(2)}) copy-start(bf16[7168,256]{1,0:T(8,128)(2,1)} %get-tuple-element.103.f_out) | copy-start | bytes 11010052 | tf_op jit(solution)/shard_map/cond
  10.2 22.1 %collective-permute-start.11 = (bf16[40,7168]{1,0:T(8,128)(2,1)S(1)}, bf16[40,7168]{1,0:T(8,128)(2,1)S(1)}, u32[]{:S(2)}, u32[]{:S(2)}) collective-permute-start(bf16[40,7168]{1,0:T(8,128)(2,1)S(1)} %get-tuple-element.107), channel_id=1, source_target_pairs={{0,1},{1,0},{2,3},{3,2},{4,5},{5,4},{6,7},{7,6},{8,9},{9,8},{10,11... | collective-permute-start | bytes 1720328 | tf_op jit(solution)/shard_map/cond/branch_1_fun/ppermute | solution.py:429
  10.4 31.7 %collective-permute-start.13 = (bf16[32,7168]{1,0:T(8,128)(2,1)S(1)}, bf16[32,7168]{1,0:T(8,128)(2,1)S(1)}, u32[]{:S(2)}, u32[]{:S(2)}) collective-permute-start(bf16[32,7168]{1,0:T(8,128)(2,1)S(1)} %get-tuple-element.109), channel_id=1, source_target_pairs={{0,1},{1,0},{2,3},{3,2},{4,5},{5,4},{6,7},{7,6},{8,9},{9,8},{10,11... | collective-permute-start | bytes 1376264 | tf_op jit(solution)/shard_map/cond/branch_1_fun/ppermute | solution.py:429
  12.3 34.0 %collective-permute-start.16 = (bf16[16,6144]{1,0:T(8,128)(2,1)S(1)}, bf16[16,6144]{1,0:T(8,128)(2,1)S(1)}, u32[]{:S(2)}, u32[]{:S(2)}) collective-permute-start(bf16[16,6144]{1,0:T(8,128)(2,1)S(1)} %get-tuple-element.112), channel_id=1, source_target_pairs={{0,1},{1,0},{2,3},{3,2},{4,5},{5,4},{6,7},{7,6},{8,9},{9,8},{10,11... | collective-permute-start | bytes 589832 | tf_op jit(solution)/shard_map/cond/branch_1_fun/ppermute | solution.py:429
  12.4 37.4 %collective-permute-start.15 = (bf16[16,5120]{1,0:T(8,128)(2,1)S(1)}, bf16[16,5120]{1,0:T(8,128)(2,1)S(1)}, u32[]{:S(2)}, u32[]{:S(2)}) collective-permute-start(bf16[16,5120]{1,0:T(8,128)(2,1)S(1)} %get-tuple-element.111), channel_id=1, source_target_pairs={{0,1},{1,0},{2,3},{3,2},{4,5},{5,4},{6,7},{7,6},{8,9},{9,8},{10,11... | collective-permute-start | bytes 491528 | tf_op jit(solution)/shard_map/cond/branch_1_fun/ppermute | solution.py:429
  33.0 21.2 %collective-permute-start.12 = (f32[40,256]{1,0:T(8,128)S(1)}, f32[40,256]{1,0:T(8,128)S(1)}, u32[]{:S(2)}, u32[]{:S(2)}) collective-permute-start(f32[40,256]{1,0:T(8,128)S(1)} %branch_1_fun.11), channel_id=1, source_target_pairs={{0,1},{1,0},{2,3},{3,2},{4,5},{5,4},{6,7},{7,6},{8,9},{9,8},{10,11... | collective-permute-start | bytes 122888 | tf_op jit(solution)/shard_map/cond/branch_1_fun/ppermute | solution.py:429
  35.1 19.1 %collective-permute-start.10 = (s16[80,256]{1,0:T(8,128)(2,1)S(1)}, s16[80,256]{1,0:T(8,128)(2,1)S(1)}, u32[]{:S(2)}, u32[]{:S(2)}) collective-permute-start(s16[80,256]{1,0:T(8,128)(2,1)S(1)} %branch_1_fun.9), channel_id=1, source_target_pairs={{0,1},{1,0},{2,3},{3,2},{4,5},{5,4},{6,7},{7,6},{8,9},{9,8},{10,11... | collective-permute-start | bytes 122888 | tf_op jit(solution)/shard_map/cond/branch_1_fun/ppermute | solution.py:429
  42.8 11.4 %collective-permute-start.14 = (f32[32,256]{1,0:T(8,128)S(1)}, f32[32,256]{1,0:T(8,128)S(1)}, u32[]{:S(2)}, u32[]{:S(2)}) collective-permute-start(f32[32,256]{1,0:T(8,128)S(1)} %branch_1_fun.12), channel_id=1, source_target_pairs={{0,1},{1,0},{2,3},{3,2},{4,5},{5,4},{6,7},{7,6},{8,9},{9,8},{10,11... | collective-permute-start | bytes 98312 | tf_op jit(solution)/shard_map/cond/branch_1_fun/ppermute | solution.py:429
  50.3 3.9 %collective-permute-start.17 = (s16[24,512]{1,0:T(8,128)(2,1)S(1)}, s16[24,512]{1,0:T(8,128)(2,1)S(1)}, u32[]{:S(2)}, u32[]{:S(2)}) collective-permute-start(s16[24,512]{1,0:T(8,128)(2,1)S(1)} %branch_1_fun.14), channel_id=1, source_target_pairs={{0,1},{1,0},{2,3},{3,2},{4,5},{5,4},{6,7},{7,6},{8,9},{9,8},{10,11... | collective-permute-start | bytes 73736 | tf_op jit(solution)/shard_map/cond/branch_1_fun/ppermute | solution.py:429
  55.2 1.2 %collective-permute-start.45 = (f32[4,8]{1,0:T(4,128)S(1)}, f32[4,8]{1,0:T(4,128)S(1)}, u32[]{:S(2)}, u32[]{:S(2)}) collective-permute-start(f32[4,8]{1,0:T(4,128)S(1)} %get-tuple-element.170), channel_id=1, source_target_pairs={{0,2},{2,0},{4,6},{6,4},{8,10},{10,8},{12,14},{14,12},{16,18},{18,... | collective-permute-start | bytes 392 | tf_op jit(solution)/shard_map/ppermute | solution.py:508
  56.4 4.6 %collective-permute-start.48 = (f32[4,8]{1,0:T(4,128)S(1)}, f32[4,8]{1,0:T(4,128)S(1)}, u32[]{:S(2)}, u32[]{:S(2)}) collective-permute-start(f32[4,8]{1,0:T(4,128)S(1)} %add.15), channel_id=1, source_target_pairs={{0,12},{2,14},{4,8},{6,10},{8,4},{10,6},{12,0},{14,2},{16,28},{18,... | collective-permute-start | bytes 392 | tf_op jit(solution)/shard_map/ppermute | solution.py:508
  59.4 3.6 %collective-permute-start.47 = (f32[4,8]{1,0:T(4,128)S(1)}, f32[4,8]{1,0:T(4,128)S(1)}, u32[]{:S(2)}, u32[]{:S(2)}) collective-permute-start(f32[4,8]{1,0:T(4,128)S(1)} %add.15), channel_id=1, source_target_pairs={{0,8},{2,10},{4,12},{6,14},{8,0},{10,2},{12,4},{14,6},{16,24},{18,... | collective-permute-start | bytes 392 | tf_op jit(solution)/shard_map/ppermute | solution.py:508
  59.9 3.6 %collective-permute-start.46 = (f32[4,8]{1,0:T(4,128)S(1)}, f32[4,8]{1,0:T(4,128)S(1)}, u32[]{:S(2)}, u32[]{:S(2)}) collective-permute-start(f32[4,8]{1,0:T(4,128)S(1)} %add.15), channel_id=1, source_target_pairs={{0,4},{2,6},{4,0},{6,2},{8,12},{10,14},{12,8},{14,10},{16,20},{18,... | collective-permute-start | bytes 392 | tf_op jit(solution)/shard_map/ppermute | solution.py:508
  63.5 4.5 %collective-permute-start.49 = (f32[4,8]{1,0:T(4,128)S(1)}, f32[4,8]{1,0:T(4,128)S(1)}, u32[]{:S(2)}, u32[]{:S(2)}) collective-permute-start(f32[4,8]{1,0:T(4,128)S(1)} %add_add_fusion), channel_id=1, source_target_pairs={{0,16},{2,18},{4,20},{6,22},{8,24},{10,26},{12,28},{14,30},{16,0},... | collective-permute-start | bytes 392 | tf_op jit(solution)/shard_map/ppermute | solution.py:508
where the time goes:
time: 68.7 us; the launch traced here: 68.6 us
  waiting for transfers between devices  29 us (42%)
  starting transfers between devices  19.8 us (29%)
  Pallas kernels  18.7 us (27%)
    ppermute x9, waiting for transfers between devices, swap(): return lax.ppermute(x, 'dp', SWAP)  22.5 us
    ppermute x9, starting transfers between devices, swap(): return lax.ppermute(x, 'dp', SWAP)  13.5 us
    pallas_call x1, Pallas kernels, own_part(): pl.pallas_call(own_kernel, out_shape=jax.ShapeDtypeStruct((rows, 2 * colu...  7.99 us
    ppermute x5, waiting for transfers between devices, layer_sum(): lax.ppermute(x, 'layer', [(i, i ^ flip) for i in range(size)])  6.5 us
    ppermute x5, starting transfers between devices, layer_sum(): lax.ppermute(x, 'layer', [(i, i ^ flip) for i in range(size)])  6.23 us
    pallas_call x1, Pallas kernels, rest_rows(): pl.pallas_call(functools.partial(rest_kernel, chunks, extra, cuts, lent),...  4.37 us
    pallas_call x1, Pallas kernels, first_rows(): pl.pallas_call(functools.partial(first_kernel, total, bounds), out_shape=...  2.64 us
    pallas_call x2, Pallas kernels, project(): pl.pallas_call(project_kernel, out_shape=jax.ShapeDtypeStruct((rows, colu...  1.47 us
  transfers between devices with their start and end apart: 14, of which 10 were waited for; matrix products, arithmetic and copies ran while one was open for 0% of the time, Pallas kernels for 22%

commit v1 on v0

--- a/solution.py
+++ b/solution.py
@@ -490,7 +490,7 @@
         large = (base + STEP) // 2 // STEP * STEP
         return rows, base, 0, [large, base - large]
     base = even - STEP
-    large = (base // 2) // STEP * STEP
+    large = (base + STEP) // 2 // STEP * STEP
     lent = lendable(base, rows - base, columns, a_wide, g_wide)
     return rows, base, lent, [large, base - STEP - large, STEP]
 

time: 68.7 us -> 69 us (level)
  no operation moved by 1% of the time
where the time goes in v1:
time: 69 us; the launch traced here: 68.6 us
  waiting for transfers between devices  29 us (42%)
  starting transfers between devices  19.8 us (29%)
  Pallas kernels  18.7 us (27%)
    ppermute x9, waiting for transfers between devices, swap(): return lax.ppermute(x, 'dp', SWAP)  22.5 us
    ppermute x9, starting transfers between devices, swap(): return lax.ppermute(x, 'dp', SWAP)  13.5 us
    pallas_call x1, Pallas kernels, own_part(): pl.pallas_call(own_kernel, out_shape=jax.ShapeDtypeStruct((rows, 2 * colu...  7.99 us
    ppermute x5, waiting for transfers between devices, layer_sum(): lax.ppermute(x, 'layer', [(i, i ^ flip) for i in range(size)])  6.5 us
    ppermute x5, starting transfers between devices, layer_sum(): lax.ppermute(x, 'layer', [(i, i ^ flip) for i in range(size)])  6.23 us
    pallas_call x1, Pallas kernels, rest_rows(): pl.pallas_call(functools.partial(rest_kernel, chunks, extra, cuts, lent),...  4.37 us
    pallas_call x1, Pallas kernels, first_rows(): pl.pallas_call(functools.partial(first_kernel, total, bounds), out_shape=...  2.64 us
    pallas_call x2, Pallas kernels, project(): pl.pallas_call(project_kernel, out_shape=jax.ShapeDtypeStruct((rows, colu...  1.47 us
  transfers between devices with their start and end apart: 14, of which 10 were waited for; matrix products, arithmetic and copies ran while one was open for 0% of the time, Pallas kernels for 22%

profile of v1, /device:TPU:0, one launch (start us, length us, event | category | flops | bytes accessed | tf_op | source)
XLA Modules:
  0.0 68.6 jit_solution(8776116135447515384)
XLA Ops:
  0.0 0.0 copy-start.14
  0.0 0.0 copy-start.5
  0.0 2.6 %shard_map.55 = (bf16[128,4096]{1,0:T(8,128)(2,1)S(1)}, s32[2]{0:T(128)S(1)}) custom-call(s32[4]{0:T(128)} %lengths_ref.1, bf16[128,8192]{1,0:T(8,128)(2,1)} %bitcast.21), custom_call_target="tpu_custom_call" | custom-call | tf_op jit(solution)/shard_map/pallas_call | solution.py:116
  2.7 0.0 copy-done.14
  2.7 0.0 copy-done.5
  2.7 52.5 %conditional.1 = (f32[4,8]{1,0:T(4,128)S(1)}) conditional(s32[]{:T(128)} %bitcast.1, (bf16[128,4096]{1,0:T(8,128)(2,1)S(1)}, s32[4]{0:T(128)S(1)}, bf16[128,8192]{1,0:T(8,128)(2,1)}, bf16[128,14336]{1,0:T(8,128)(2,1)}, bf16[4096,256]{1,0:T(8,128)(2,1)S(1)}, /*index=5*/bf16[7168,256]{1,0:T(8,128)(2,1)}, ...), branch_computations={%region_0.0_spmd, %region_1.0_spmd, %region_2.0_spmd, %region_3.0_... | conditional | flops 2900000000 | bytes 49304004 | solution.py:524
  2.7 0.0 copy-start.7
  2.8 3.0 %collective-permute-start.9 = (bf16[72,4096]{1,0:T(8,128)(2,1)S(1)}, bf16[72,4096]{1,0:T(8,128)(2,1)S(1)}, u32[]{:S(2)}, u32[]{:S(2)}) collective-permute-start(bf16[72,4096]{1,0:T(8,128)(2,1)S(1)} %slice.13), channel_id=1, source_target_pairs={{0,1},{1,0},{2,3},{3,2},{4,5},{5,4},{6,7},{7,6},{8,9},{9,8},{10,11... | collective-permute-start | bytes 1769480 | tf_op jit(solution)/shard_map/cond/branch_1_fun/ppermute | solution.py:429
  5.8 0.0 copy-start.1
  5.8 4.4 %branch_1_fun.10 = (bf16[40,7168]{1,0:T(8,128)(2,1)S(1)}, bf16[32,7168]{1,0:T(8,128)(2,1)S(1)}, bf16[16,6144]{1,0:T(8,128)(2,1)S(1)}, bf16[16,5120]{1,0:T(8,128)(2,1)S(1)}) custom-call(s32[2]{0:T(128)S(1)} %get-tuple-element.106.flags_ref, s32[4]{0:T(128)S(1)} %get-tuple-element.98.lengths_ref._, bf16[128,4096]{1,0:T(8,128)(2,1)S(1)} %get-tuple-element.99.act, ...), custom_call_target="tpu_custom_call" | custom-call | tf_op jit(solution)/shard_map/cond/branch_1_fun/pallas_call | solution.py:185
  10.2 0.2 collective-permute-start.11
  10.4 1.9 %collective-permute-start.13 = (bf16[32,7168]{1,0:T(8,128)(2,1)S(1)}, bf16[32,7168]{1,0:T(8,128)(2,1)S(1)}, u32[]{:S(2)}, u32[]{:S(2)}) collective-permute-start(bf16[32,7168]{1,0:T(8,128)(2,1)S(1)} %get-tuple-element.109), channel_id=1, source_target_pairs={{0,1},{1,0},{2,3},{3,2},{4,5},{5,4},{6,7},{7,6},{8,9},{9,8},{10,11... | collective-permute-start | bytes 1376264 | tf_op jit(solution)/shard_map/cond/branch_1_fun/ppermute | solution.py:429
  12.3 0.1 collective-permute-start.16
  12.4 1.9 %collective-permute-start.15 = (bf16[16,5120]{1,0:T(8,128)(2,1)S(1)}, bf16[16,5120]{1,0:T(8,128)(2,1)S(1)}, u32[]{:S(2)}, u32[]{:S(2)}) collective-permute-start(bf16[16,5120]{1,0:T(8,128)(2,1)S(1)} %get-tuple-element.111), channel_id=1, source_target_pairs={{0,1},{1,0},{2,3},{3,2},{4,5},{5,4},{6,7},{7,6},{8,9},{9,8},{10,11... | collective-permute-start | bytes 491528 | tf_op jit(solution)/shard_map/cond/branch_1_fun/ppermute | solution.py:429
  14.3 0.0 copy-done.7
  14.3 0.0 copy-done.1
  14.3 8.0 %branch_1_fun.8.rest_0_ = f32[88,512]{1,0:T(8,128)S(1)} custom-call(s32[4]{0:T(128)S(1)} %get-tuple-element.98.lengths_ref._, bf16[128,8192]{1,0:T(8,128)(2,1)} %get-tuple-element.100.act_ref, bf16[128,14336]{1,0:T(8,128)(2,1)S(1)} %copy-done.7, bf16[4096,256]{1,0:T(8,128)(2,1)S(1)} %get-tuple-element.102.f_in, bf16[7168,256]{1,0:T(8,128)(2,1)S(1)} %copy-done.1, ...), custom_call_target="tpu_custom_call" | custom-call | tf_op jit(solution)/shard_map/cond/branch_1_fun/pallas_call | solution.py:221
  22.3 0.0 collective-permute-done.9.x_ref
  22.3 0.5 branch_1_fun.9
  22.9 9.4 %collective-permute-done.11.x_ref = bf16[40,7168]{1,0:T(8,128)(2,1)S(1)} collective-permute-done((bf16[40,7168]{1,0:T(8,128)(2,1)S(1)}, bf16[40,7168]{1,0:T(8,128)(2,1)S(1)}, u32[]{:S(2)}, u32[]{:S(2)}) %collective-permute-start.11) | collective-permute-done | bytes 573472 | tf_op jit(solution)/shard_map/cond/branch_1_fun/ppermute | solution.py:429
  32.3 0.7 %branch_1_fun.11 = f32[40,256]{1,0:T(8,128)S(1)} custom-call(bf16[40,7168]{1,0:T(8,128)(2,1)S(1)} %collective-permute-done.11.x_ref, bf16[7168,256]{1,0:T(8,128)(2,1)S(1)} %copy-done.1), custom_call_target="tpu_custom_call" | custom-call | tf_op jit(solution)/shard_map/cond/branch_1_fun/pallas_call | solution.py:276
  33.0 2.1 %collective-permute-start.12 = (f32[40,256]{1,0:T(8,128)S(1)}, f32[40,256]{1,0:T(8,128)S(1)}, u32[]{:S(2)}, u32[]{:S(2)}) collective-permute-start(f32[40,256]{1,0:T(8,128)S(1)} %branch_1_fun.11), channel_id=1, source_target_pairs={{0,1},{1,0},{2,3},{3,2},{4,5},{5,4},{6,7},{7,6},{8,9},{9,8},{10,11... | collective-permute-start | bytes 122888 | tf_op jit(solution)/shard_map/cond/branch_1_fun/ppermute | solution.py:429
  35.1 0.1 collective-permute-start.10
  35.2 6.9 %collective-permute-done.13.x_ref = bf16[32,7168]{1,0:T(8,128)(2,1)S(1)} collective-permute-done((bf16[32,7168]{1,0:T(8,128)(2,1)S(1)}, bf16[32,7168]{1,0:T(8,128)(2,1)S(1)}, u32[]{:S(2)}, u32[]{:S(2)}) %collective-permute-start.13) | collective-permute-done | bytes 458784 | tf_op jit(solution)/shard_map/cond/branch_1_fun/ppermute | solution.py:429
  42.1 0.7 %branch_1_fun.12 = f32[32,256]{1,0:T(8,128)S(1)} custom-call(bf16[32,7168]{1,0:T(8,128)(2,1)S(1)} %collective-permute-done.13.x_ref, bf16[7168,256]{1,0:T(8,128)(2,1)S(1)} %copy-done.1), custom_call_target="tpu_custom_call" | custom-call | tf_op jit(solution)/shard_map/cond/branch_1_fun/pallas_call | solution.py:276
  42.8 2.1 %collective-permute-start.14 = (f32[32,256]{1,0:T(8,128)S(1)}, f32[32,256]{1,0:T(8,128)S(1)}, u32[]{:S(2)}, u32[]{:S(2)}) collective-permute-start(f32[32,256]{1,0:T(8,128)S(1)} %branch_1_fun.12), channel_id=1, source_target_pairs={{0,1},{1,0},{2,3},{3,2},{4,5},{5,4},{6,7},{7,6},{8,9},{9,8},{10,11... | collective-permute-start | bytes 98312 | tf_op jit(solution)/shard_map/cond/branch_1_fun/ppermute | solution.py:429
  44.9 1.4 %collective-permute-done.16.x_ref = bf16[16,6144]{1,0:T(8,128)(2,1)S(1)} collective-permute-done((bf16[16,6144]{1,0:T(8,128)(2,1)S(1)}, bf16[16,6144]{1,0:T(8,128)(2,1)S(1)}, u32[]{:S(2)}, u32[]{:S(2)}) %collective-permute-start.16) | collective-permute-done | bytes 196640 | tf_op jit(solution)/shard_map/cond/branch_1_fun/ppermute | solution.py:429
  46.3 0.5 branch_1_fun.13.made
  46.8 3.0 %collective-permute-done.15.x_ref = bf16[16,5120]{1,0:T(8,128)(2,1)S(1)} collective-permute-done((bf16[16,5120]{1,0:T(8,128)(2,1)S(1)}, bf16[16,5120]{1,0:T(8,128)(2,1)S(1)}, u32[]{:S(2)}, u32[]{:S(2)}) %collective-permute-start.15) | collective-permute-done | bytes 163872 | tf_op jit(solution)/shard_map/cond/branch_1_fun/ppermute | solution.py:429
  49.8 0.5 branch_1_fun.14
  50.3 2.1 %collective-permute-start.17 = (s16[24,512]{1,0:T(8,128)(2,1)S(1)}, s16[24,512]{1,0:T(8,128)(2,1)S(1)}, u32[]{:S(2)}, u32[]{:S(2)}) collective-permute-start(s16[24,512]{1,0:T(8,128)(2,1)S(1)} %branch_1_fun.14), channel_id=1, source_target_pairs={{0,1},{1,0},{2,3},{3,2},{4,5},{5,4},{6,7},{7,6},{8,9},{9,8},{10,11... | collective-permute-start | bytes 73736 | tf_op jit(solution)/shard_map/cond/branch_1_fun/ppermute | solution.py:429
  52.4 1.8 %collective-permute-done.17.rest_4_ = s16[24,512]{1,0:T(8,128)(2,1)S(1)} collective-permute-done((s16[24,512]{1,0:T(8,128)(2,1)S(1)}, s16[24,512]{1,0:T(8,128)(2,1)S(1)}, u32[]{:S(2)}, u32[]{:S(2)}) %collective-permute-start.17) | collective-permute-done | bytes 24608 | tf_op jit(solution)/shard_map/cond/branch_1_fun/ppermute | solution.py:429
  54.2 0.0 collective-permute-done.14.rest_3_
  54.2 0.0 collective-permute-done.12.rest_2_
  54.2 0.0 collective-permute-done.10.rest_1_
  54.2 0.8 %branch_1_fun.15 = f32[4,8]{1,0:T(4,128)S(1)} custom-call(s32[4]{0:T(128)S(1)} %get-tuple-element.98.lengths_ref._, f32[88,512]{1,0:T(8,128)S(1)} %branch_1_fun.8.rest_0_, s16[80,256]{1,0:T(8,128)(2,1)S(1)} %collective-permute-done.10.rest_1_, f32[40,256]{1,0:T(8,128)S(1)} %collective-permute-done.12.rest_2_, f32[32,256]{1,0:T(8,128)S(1)} %collective-permute-done.14.rest_3_, ...), custom_call_target="tpu_custom_call" | custom-call | tf_op jit(solution)/shard_map/cond/branch_1_fun/pallas_call | solution.py:410
  55.2 0.1 collective-permute-start.45
  55.3 1.1 %collective-permute-done.45 = f32[4,8]{1,0:T(4,128)S(1)} collective-permute-done((f32[4,8]{1,0:T(4,128)S(1)}, f32[4,8]{1,0:T(4,128)S(1)}, u32[]{:S(2)}, u32[]{:S(2)}) %collective-permute-start.45) | collective-permute-done | bytes 160 | tf_op jit(solution)/shard_map/ppermute | solution.py:508
  56.4 3.0 %collective-permute-start.48 = (f32[4,8]{1,0:T(4,128)S(1)}, f32[4,8]{1,0:T(4,128)S(1)}, u32[]{:S(2)}, u32[]{:S(2)}) collective-permute-start(f32[4,8]{1,0:T(4,128)S(1)} %add.15), channel_id=1, source_target_pairs={{0,12},{2,14},{4,8},{6,10},{8,4},{10,6},{12,0},{14,2},{16,28},{18,... | collective-permute-start | bytes 392 | tf_op jit(solution)/shard_map/ppermute | solution.py:508
  59.4 0.4 collective-permute-start.47
  59.9 0.1 collective-permute-start.46
  60.0 1.0 %collective-permute-done.48 = f32[4,8]{1,0:T(4,128)S(1)} collective-permute-done((f32[4,8]{1,0:T(4,128)S(1)}, f32[4,8]{1,0:T(4,128)S(1)}, u32[]{:S(2)}, u32[]{:S(2)}) %collective-permute-start.48) | collective-permute-done | bytes 160 | tf_op jit(solution)/shard_map/ppermute | solution.py:508
  61.0 2.0 %collective-permute-done.47 = f32[4,8]{1,0:T(4,128)S(1)} collective-permute-done((f32[4,8]{1,0:T(4,128)S(1)}, f32[4,8]{1,0:T(4,128)S(1)}, u32[]{:S(2)}, u32[]{:S(2)}) %collective-permute-start.47) | collective-permute-done | bytes 160 | tf_op jit(solution)/shard_map/ppermute | solution.py:508
  63.0 0.4 collective-permute-done.46
  63.5 2.6 %collective-permute-start.49 = (f32[4,8]{1,0:T(4,128)S(1)}, f32[4,8]{1,0:T(4,128)S(1)}, u32[]{:S(2)}, u32[]{:S(2)}) collective-permute-start(f32[4,8]{1,0:T(4,128)S(1)} %add_add_fusion), channel_id=1, source_target_pairs={{0,16},{2,18},{4,20},{6,22},{8,24},{10,26},{12,28},{14,30},{16,0},... | collective-permute-start | bytes 392 | tf_op jit(solution)/shard_map/ppermute | solution.py:508
  66.1 1.9 %collective-permute-done.49 = f32[4,8]{1,0:T(4,128)S(1)} collective-permute-done((f32[4,8]{1,0:T(4,128)S(1)}, f32[4,8]{1,0:T(4,128)S(1)}, u32[]{:S(2)}, u32[]{:S(2)}) %collective-permute-start.49) | collective-permute-done | bytes 160 | tf_op jit(solution)/shard_map/ppermute | solution.py:508
  68.0 0.6 add_multiply_fusion
  (3 shorter events, 0.0 us)
Async XLA Ops:
  0.0 2.7 %copy-start.14 = (s32[4]{0:T(128)S(1)}, s32[4]{0:T(128)}, u32[]{:S(2)}) copy-start(s32[4]{0:T(128)} %lengths_ref.1) | copy-start | bytes 52
  0.0 2.7 %copy-start.5 = (bf16[1,4096,256]{2,1,0:T(8,128)(2,1)S(1)}, bf16[1,4096,256]{2,1,0:T(8,128)(2,1)}, u32[]{:S(2)}) copy-start(bf16[1,4096,256]{2,1,0:T(8,128)(2,1)} %param.12) | copy-start | bytes 6291460
  2.7 11.6 %copy-start.7 = (bf16[128,14336]{1,0:T(8,128)(2,1)S(1)}, bf16[128,14336]{1,0:T(8,128)(2,1)}, u32[]{:S(2)}) copy-start(bf16[128,14336]{1,0:T(8,128)(2,1)} %get-tuple-element.101.grad_ref) | copy-start | bytes 11010052 | tf_op jit(solution)/shard_map/cond
  2.8 19.5 %collective-permute-start.9 = (bf16[72,4096]{1,0:T(8,128)(2,1)S(1)}, bf16[72,4096]{1,0:T(8,128)(2,1)S(1)}, u32[]{:S(2)}, u32[]{:S(2)}) collective-permute-start(bf16[72,4096]{1,0:T(8,128)(2,1)S(1)} %slice.13), channel_id=1, source_target_pairs={{0,1},{1,0},{2,3},{3,2},{4,5},{5,4},{6,7},{7,6},{8,9},{9,8},{10,11... | collective-permute-start | bytes 1769480 | tf_op jit(solution)/shard_map/cond/branch_1_fun/ppermute | solution.py:429
  5.8 8.5 %copy-start.1 = (bf16[7168,256]{1,0:T(8,128)(2,1)S(1)}, bf16[7168,256]{1,0:T(8,128)(2,1)}, u32[]{:S(2)}) copy-start(bf16[7168,256]{1,0:T(8,128)(2,1)} %get-tuple-element.103.f_out) | copy-start | bytes 11010052 | tf_op jit(solution)/shard_map/cond
  10.2 22.1 %collective-permute-start.11 = (bf16[40,7168]{1,0:T(8,128)(2,1)S(1)}, bf16[40,7168]{1,0:T(8,128)(2,1)S(1)}, u32[]{:S(2)}, u32[]{:S(2)}) collective-permute-start(bf16[40,7168]{1,0:T(8,128)(2,1)S(1)} %get-tuple-element.107), channel_id=1, source_target_pairs={{0,1},{1,0},{2,3},{3,2},{4,5},{5,4},{6,7},{7,6},{8,9},{9,8},{10,11... | collective-permute-start | bytes 1720328 | tf_op jit(solution)/shard_map/cond/branch_1_fun/ppermute | solution.py:429
  10.4 31.7 %collective-permute-start.13 = (bf16[32,7168]{1,0:T(8,128)(2,1)S(1)}, bf16[32,7168]{1,0:T(8,128)(2,1)S(1)}, u32[]{:S(2)}, u32[]{:S(2)}) collective-permute-start(bf16[32,7168]{1,0:T(8,128)(2,1)S(1)} %get-tuple-element.109), channel_id=1, source_target_pairs={{0,1},{1,0},{2,3},{3,2},{4,5},{5,4},{6,7},{7,6},{8,9},{9,8},{10,11... | collective-permute-start | bytes 1376264 | tf_op jit(solution)/shard_map/cond/branch_1_fun/ppermute | solution.py:429
  12.3 34.0 %collective-permute-start.16 = (bf16[16,6144]{1,0:T(8,128)(2,1)S(1)}, bf16[16,6144]{1,0:T(8,128)(2,1)S(1)}, u32[]{:S(2)}, u32[]{:S(2)}) collective-permute-start(bf16[16,6144]{1,0:T(8,128)(2,1)S(1)} %get-tuple-element.112), channel_id=1, source_target_pairs={{0,1},{1,0},{2,3},{3,2},{4,5},{5,4},{6,7},{7,6},{8,9},{9,8},{10,11... | collective-permute-start | bytes 589832 | tf_op jit(solution)/shard_map/cond/branch_1_fun/ppermute | solution.py:429
  12.4 37.4 %collective-permute-start.15 = (bf16[16,5120]{1,0:T(8,128)(2,1)S(1)}, bf16[16,5120]{1,0:T(8,128)(2,1)S(1)}, u32[]{:S(2)}, u32[]{:S(2)}) collective-permute-start(bf16[16,5120]{1,0:T(8,128)(2,1)S(1)} %get-tuple-element.111), channel_id=1, source_target_pairs={{0,1},{1,0},{2,3},{3,2},{4,5},{5,4},{6,7},{7,6},{8,9},{9,8},{10,11... | collective-permute-start | bytes 491528 | tf_op jit(solution)/shard_map/cond/branch_1_fun/ppermute | solution.py:429
  33.0 21.2 %collective-permute-start.12 = (f32[40,256]{1,0:T(8,128)S(1)}, f32[40,256]{1,0:T(8,128)S(1)}, u32[]{:S(2)}, u32[]{:S(2)}) collective-permute-start(f32[40,256]{1,0:T(8,128)S(1)} %branch_1_fun.11), channel_id=1, source_target_pairs={{0,1},{1,0},{2,3},{3,2},{4,5},{5,4},{6,7},{7,6},{8,9},{9,8},{10,11... | collective-permute-start | bytes 122888 | tf_op jit(solution)/shard_map/cond/branch_1_fun/ppermute | solution.py:429
  35.1 19.1 %collective-permute-start.10 = (s16[80,256]{1,0:T(8,128)(2,1)S(1)}, s16[80,256]{1,0:T(8,128)(2,1)S(1)}, u32[]{:S(2)}, u32[]{:S(2)}) collective-permute-start(s16[80,256]{1,0:T(8,128)(2,1)S(1)} %branch_1_fun.9), channel_id=1, source_target_pairs={{0,1},{1,0},{2,3},{3,2},{4,5},{5,4},{6,7},{7,6},{8,9},{9,8},{10,11... | collective-permute-start | bytes 122888 | tf_op jit(solution)/shard_map/cond/branch_1_fun/ppermute | solution.py:429
  42.8 11.4 %collective-permute-start.14 = (f32[32,256]{1,0:T(8,128)S(1)}, f32[32,256]{1,0:T(8,128)S(1)}, u32[]{:S(2)}, u32[]{:S(2)}) collective-permute-start(f32[32,256]{1,0:T(8,128)S(1)} %branch_1_fun.12), channel_id=1, source_target_pairs={{0,1},{1,0},{2,3},{3,2},{4,5},{5,4},{6,7},{7,6},{8,9},{9,8},{10,11... | collective-permute-start | bytes 98312 | tf_op jit(solution)/shard_map/cond/branch_1_fun/ppermute | solution.py:429
  50.3 3.9 %collective-permute-start.17 = (s16[24,512]{1,0:T(8,128)(2,1)S(1)}, s16[24,512]{1,0:T(8,128)(2,1)S(1)}, u32[]{:S(2)}, u32[]{:S(2)}) collective-permute-start(s16[24,512]{1,0:T(8,128)(2,1)S(1)} %branch_1_fun.14), channel_id=1, source_target_pairs={{0,1},{1,0},{2,3},{3,2},{4,5},{5,4},{6,7},{7,6},{8,9},{9,8},{10,11... | collective-permute-start | bytes 73736 | tf_op jit(solution)/shard_map/cond/branch_1_fun/ppermute | solution.py:429
  55.2 1.2 %collective-permute-start.45 = (f32[4,8]{1,0:T(4,128)S(1)}, f32[4,8]{1,0:T(4,128)S(1)}, u32[]{:S(2)}, u32[]{:S(2)}) collective-permute-start(f32[4,8]{1,0:T(4,128)S(1)} %get-tuple-element.170), channel_id=1, source_target_pairs={{0,2},{2,0},{4,6},{6,4},{8,10},{10,8},{12,14},{14,12},{16,18},{18,... | collective-permute-start | bytes 392 | tf_op jit(solution)/shard_map/ppermute | solution.py:508
  56.4 4.6 %collective-permute-start.48 = (f32[4,8]{1,0:T(4,128)S(1)}, f32[4,8]{1,0:T(4,128)S(1)}, u32[]{:S(2)}, u32[]{:S(2)}) collective-permute-start(f32[4,8]{1,0:T(4,128)S(1)} %add.15), channel_id=1, source_target_pairs={{0,12},{2,14},{4,8},{6,10},{8,4},{10,6},{12,0},{14,2},{16,28},{18,... | collective-permute-start | bytes 392 | tf_op jit(solution)/shard_map/ppermute | solution.py:508
  59.4 3.6 %collective-permute-start.47 = (f32[4,8]{1,0:T(4,128)S(1)}, f32[4,8]{1,0:T(4,128)S(1)}, u32[]{:S(2)}, u32[]{:S(2)}) collective-permute-start(f32[4,8]{1,0:T(4,128)S(1)} %add.15), channel_id=1, source_target_pairs={{0,8},{2,10},{4,12},{6,14},{8,0},{10,2},{12,4},{14,6},{16,24},{18,... | collective-permute-start | bytes 392 | tf_op jit(solution)/shard_map/ppermute | solution.py:508
  59.9 3.6 %collective-permute-start.46 = (f32[4,8]{1,0:T(4,128)S(1)}, f32[4,8]{1,0:T(4,128)S(1)}, u32[]{:S(2)}, u32[]{:S(2)}) collective-permute-start(f32[4,8]{1,0:T(4,128)S(1)} %add.15), channel_id=1, source_target_pairs={{0,4},{2,6},{4,0},{6,2},{8,12},{10,14},{12,8},{14,10},{16,20},{18,... | collective-permute-start | bytes 392 | tf_op jit(solution)/shard_map/ppermute | solution.py:508
  63.5 4.5 %collective-permute-start.49 = (f32[4,8]{1,0:T(4,128)S(1)}, f32[4,8]{1,0:T(4,128)S(1)}, u32[]{:S(2)}, u32[]{:S(2)}) collective-permute-start(f32[4,8]{1,0:T(4,128)S(1)} %add_add_fusion), channel_id=1, source_target_pairs={{0,16},{2,18},{4,20},{6,22},{8,24},{10,26},{12,28},{14,30},{16,0},... | collective-permute-start | bytes 392 | tf_op jit(solution)/shard_map/ppermute | solution.py:508
